TPU v7x, 32 devices: a whole 2x2x4 slice. The times are simulated.
32 devices in a mesh: len: 4 (over y, x), hgt: 4 (over z), wid: 2 (over core).
Axes of the slice: x: 2, y: 2, z: 4, core: 2. Of those that a mesh axis runs over, the one named last changes fastest.
Arguments:
- precursor_velocity: float32 [3, 64, 32, 128], P(None, 'len', 'hgt'), may hold values from -6 to 6
- face_velocity: float32 [3, 64, 32, 256], P(None, 'len', 'hgt', 'wid'), may hold values from -6 to 6
- solid_cells: int32 [64, 32, 256], P('len', 'hgt', 'wid'), may hold values 0 or 1
- inlet_profile: float32 [3, 32], P(None, 'hgt'), may hold values from -6 to 6
- target_spread: float32 [3, 32], P(None, 'hgt'), may hold values from 0.3 to 2
Outputs:
- precursor_next: float32 [3, 64, 32, 128], P(None, 'len', 'hgt')
- face_next: float32 [3, 64, 32, 256], P(None, 'len', 'hgt', 'wid')
All inputs are finite; a program needn't handle non-finite values. No bound on the sum of `solid_cells` on one device may be relied on, other than what follows from the above.
Results may differ from a plain program's by a relative error of at most 0.0001.
Values sent between devices are 32-bit elements; how exact they have to be, the bound alone decides.
A program may use at most 64 MiB of HBM per device.

v0:
```python
import jax
import jax.numpy as jnp
from jax import lax
from jax.sharding import PartitionSpec as P

STEPS = 3


time_step = 0.3
viscosity = 0.04
smag_coef = 0.03
spread_eps = 1e-05


def padded_2(x, sides, width, wrap):
    for axis, dim in sides:
        devices, length = (lax.axis_size(axis), x.shape[dim])
        up = [(i, (i + 1) % devices) for i in range(devices if wrap else devices - 1)]
        down = [(j, i) for i, j in up]
        last = lax.slice_in_dim(x, length - width, length, axis=dim)
        leading = lax.slice_in_dim(x, 0, width, axis=dim)
        before = lax.ppermute(last, axis, up)
        after = lax.ppermute(leading, axis, down)
        x = jnp.concatenate([before, x, after], axis=dim)
    return x


def stencil(velocity, ext_len, ext_hgt, ext_wid):
    extended = (ext_len, ext_hgt, ext_wid)
    gradients = []
    laplacian = jnp.zeros_like(velocity)
    for axis_dim in range(3):
        source = extended[axis_dim]
        total = source.shape[axis_dim + 1]
        upper_side = lax.slice_in_dim(source, 2, total, axis=axis_dim + 1)
        lower_side = lax.slice_in_dim(source, 0, total - 2, axis=axis_dim + 1)
        gradients.append((upper_side - lower_side) * 0.5)
        laplacian = laplacian + upper_side + lower_side - 2.0 * velocity
    strain_sum = jnp.zeros_like(velocity[0])
    for comp in range(3):
        for axis_dim in range(3):
            strain = 0.5 * (gradients[axis_dim][comp] + gradients[comp][axis_dim])
            strain_sum = strain_sum + strain * strain
    strain_norm = jnp.sqrt(2.0 * strain_sum)
    nu_eff = viscosity + smag_coef * strain_norm
    advect = jnp.zeros_like(velocity)
    for axis_dim in range(3):
        advect = advect + velocity[axis_dim][None] * gradients[axis_dim]
    return velocity + time_step * (nu_eff[None] * laplacian - advect)


def rescale_plane(recycled, inlet_profile, target_spread):
    plane_mean = jnp.mean(recycled, axis=2, keepdims=True)
    fluctuation = recycled - plane_mean
    plane_spread = jnp.sqrt(jnp.mean(fluctuation * fluctuation, axis=2, keepdims=True) + spread_eps)
    return inlet_profile[:, :, None] + target_spread[:, :, None] / plane_spread * fluctuation


def on_device(precursor_velocity, face_velocity, solid_cells, inlet_profile, target_spread):
    len_index = lax.axis_index("len")
    len_count = lax.axis_size("len")
    fluid_share = (1 - solid_cells).astype(jnp.float32)
    precursor = precursor_velocity
    face_zone = face_velocity
    for step_index in range(STEPS):
        pre_len = padded_2(precursor, (("len", 1),), 1, True)
        pre_hgt = padded_2(precursor, (("hgt", 2),), 1, False)
        pre_wid = jnp.pad(precursor, ((0, 0), (0, 0), (0, 0), (1, 1)))
        recycled = pre_len[:, 0]
        inlet_plane = rescale_plane(recycled, inlet_profile, target_spread)
        inlet_plane = jnp.tile(inlet_plane, (1, 1, face_zone.shape[3] // recycled.shape[2]))
        padded = padded_2(face_zone, (("len", 1), ("hgt", 2), ("wid", 3)), 1, False)
        face_len = padded[:, :, 1:-1, 1:-1]
        inlet_side = jnp.where(len_index == 0, inlet_plane, face_len[:, 0])
        outlet_side = jnp.where(len_index == len_count - 1, face_zone[:, -1], face_len[:, -1])
        face_len = jnp.concatenate(
            [inlet_side[:, None], face_len[:, 1:-1], outlet_side[:, None]], axis=1
        )
        face_hgt = padded[:, 1:-1, :, 1:-1]
        face_wid = padded[:, 1:-1, 1:-1, :]
        face_new = stencil(face_zone, face_len, face_hgt, face_wid) * fluid_share[None]
        wid_count = lax.axis_size("wid")
        row_count = precursor.shape[1] // wid_count
        row_start = lax.axis_index("wid") * row_count
        own_rows = stencil(
            lax.dynamic_slice_in_dim(precursor, row_start, row_count, 1),
            lax.dynamic_slice_in_dim(pre_len, row_start, row_count + 2, 1),
            lax.dynamic_slice_in_dim(pre_hgt, row_start, row_count, 1),
            lax.dynamic_slice_in_dim(pre_wid, row_start, row_count, 1),
        )
        precursor = lax.all_gather(own_rows, "wid", axis=1, tiled=True)
        face_zone = face_new
    return (precursor, face_zone)


def solution(mesh):
    return jax.shard_map(
        on_device,
        mesh=mesh,
        in_specs=(
            P(None, "len", "hgt", None),
            P(None, "len", "hgt", "wid"),
            P("len", "hgt", "wid"),
            P(None, "hgt"),
            P(None, "hgt"),
        ),
        out_specs=(P(None, "len", "hgt", None), P(None, "len", "hgt", "wid")),
        check_vma=False,
    )
```

profile of v0, /device:TPU:29, one launch (start us, length us, event | category | flops | bytes accessed | tf_op | source)
XLA Modules:
  0.0 118.3 jit_solution(5130794436268835584)
XLA Ops:
  1.7 1.3 %collective-permute-start.2 = (f32[3,16,1,128]{3,2,1,0:T(1,128)S(1)}, f32[3,16,1,128]{3,2,1,0:T(1,128)S(1)}, u32[]{:S(2)}, u32[]{:S(2)}) collective-permute-start(f32[3,16,1,128]{3,2,1,0:T(1,128)S(1)} %get-tuple-element.57), channel_id=1, source_target_pairs={{0,2},{2,4},{4,6},{1,3},{3,5},{5,7},{8,10},{10,12},{12,14},{9,11},... | collective-permute-start | bytes 73736 | tf_op jit(solution)/shard_map/ppermute | solution.py:22
  3.0 4.0 %collective-permute-start.3 = (f32[3,16,1,128]{3,2,1,0:T(1,128)S(1)}, f32[3,16,1,128]{3,2,1,0:T(1,128)S(1)}, u32[]{:S(2)}, u32[]{:S(2)}) collective-permute-start(f32[3,16,1,128]{3,2,1,0:T(1,128)S(1)} %get-tuple-element.56), channel_id=1, source_target_pairs={{2,0},{4,2},{6,4},{3,1},{5,3},{7,5},{10,8},{12,10},{14,12},{11,9},... | collective-permute-start | bytes 73736 | tf_op jit(solution)/shard_map/ppermute | solution.py:23
  10.8 2.2 %collective-permute-start.12 = (f32[3,1,8,128]{3,2,1,0:T(8,128)S(1)}, f32[3,1,8,128]{3,2,1,0:T(8,128)S(1)}, u32[]{:S(2)}, u32[]{:S(2)}) collective-permute-start(f32[3,1,8,128]{3,2,1,0:T(8,128)S(1)} %slice.574), channel_id=1, source_target_pairs={{8,0},{16,8},{24,16},{9,1},{17,9},{25,17},{10,2},{18,10},{26,18},{... | collective-permute-start | bytes 36872 | tf_op jit(solution)/shard_map/ppermute | solution.py:23
  15.2 3.0 %collective-permute-start.13 = (f32[3,1,8,128]{3,2,1,0:T(8,128)S(1)}, f32[3,1,8,128]{3,2,1,0:T(8,128)S(1)}, u32[]{:S(2)}, u32[]{:S(2)}) collective-permute-start(f32[3,1,8,128]{3,2,1,0:T(8,128)S(1)} %get-tuple-element.35), channel_id=1, source_target_pairs={{0,8},{8,16},{16,24},{1,9},{9,17},{17,25},{2,10},{10,18},{18,26},{... | collective-permute-start | bytes 36872 | tf_op jit(solution)/shard_map/ppermute | solution.py:22
  18.7 3.9 %all_gather.9 = f32[3,16,8,128]{3,2,1,0:T(8,128)S(1)} all-gather(f32[3,8,8,128]{3,2,1,0:T(8,128)S(1)} %multiply_add_fusion.2), channel_id=1, replica_groups=mesh['len'=4,'hgt'=4,'wid'=2] {'wid'}, dimensions={1}, use_global_device_ids=true | all-gather | bytes 294912 | tf_op jit(solution)/shard_map/all_gather | solution.py:91
  22.9 2.4 %collective-permute-start.5 = (f32[3,1,8,128]{3,2,1,0:T(8,128)S(1)}, f32[3,1,8,128]{3,2,1,0:T(8,128)S(1)}, u32[]{:S(2)}, u32[]{:S(2)}) collective-permute-start(f32[3,1,8,128]{3,2,1,0:T(8,128)S(1)} %get-tuple-element.47), channel_id=1, source_target_pairs={{8,0},{16,8},{24,16},{0,24},{9,1},{17,9},{25,17},{1,25},{10,2},{18... | collective-permute-start | bytes 36872 | tf_op jit(solution)/shard_map/ppermute | solution.py:23
  25.3 1.3 %collective-permute-start.6 = (f32[3,16,1,128]{3,2,1,0:T(1,128)S(1)}, f32[3,16,1,128]{3,2,1,0:T(1,128)S(1)}, u32[]{:S(2)}, u32[]{:S(2)}) collective-permute-start(f32[3,16,1,128]{3,2,1,0:T(1,128)S(1)} %get-tuple-element.50), channel_id=1, source_target_pairs={{0,2},{2,4},{4,6},{1,3},{3,5},{5,7},{8,10},{10,12},{12,14},{9,11},... | collective-permute-start | bytes 73736 | tf_op jit(solution)/shard_map/ppermute | solution.py:22
  26.6 4.0 %collective-permute-start.7 = (f32[3,16,1,128]{3,2,1,0:T(1,128)S(1)}, f32[3,16,1,128]{3,2,1,0:T(1,128)S(1)}, u32[]{:S(2)}, u32[]{:S(2)}) collective-permute-start(f32[3,16,1,128]{3,2,1,0:T(1,128)S(1)} %get-tuple-element.49), channel_id=1, source_target_pairs={{2,0},{4,2},{6,4},{3,1},{5,3},{7,5},{10,8},{12,10},{14,12},{11,9},... | collective-permute-start | bytes 73736 | tf_op jit(solution)/shard_map/ppermute | solution.py:23
  31.8 3.6 %all_gather.10 = f32[3,16,8,128]{3,2,1,0:T(8,128)S(1)} all-gather(f32[3,8,8,128]{3,2,1,0:T(8,128)S(1)} %multiply_add_fusion.1), channel_id=1, replica_groups=mesh['len'=4,'hgt'=4,'wid'=2] {'wid'}, dimensions={1}, use_global_device_ids=true | all-gather | bytes 294912 | tf_op jit(solution)/shard_map/all_gather | solution.py:91
  35.7 2.4 %collective-permute-start.9 = (f32[3,1,8,128]{3,2,1,0:T(8,128)S(1)}, f32[3,1,8,128]{3,2,1,0:T(8,128)S(1)}, u32[]{:S(2)}, u32[]{:S(2)}) collective-permute-start(f32[3,1,8,128]{3,2,1,0:T(8,128)S(1)} %get-tuple-element.40), channel_id=1, source_target_pairs={{8,0},{16,8},{24,16},{0,24},{9,1},{17,9},{25,17},{1,25},{10,2},{18... | collective-permute-start | bytes 36872 | tf_op jit(solution)/shard_map/ppermute | solution.py:23
  39.4 4.6 %collective-permute-start.11 = (f32[3,16,1,128]{3,2,1,0:T(1,128)S(1)}, f32[3,16,1,128]{3,2,1,0:T(1,128)S(1)}, u32[]{:S(2)}, u32[]{:S(2)}) collective-permute-start(f32[3,16,1,128]{3,2,1,0:T(1,128)S(1)} %get-tuple-element.42), channel_id=1, source_target_pairs={{2,0},{4,2},{6,4},{3,1},{5,3},{7,5},{10,8},{12,10},{14,12},{11,9},... | collective-permute-start | bytes 73736 | tf_op jit(solution)/shard_map/ppermute | solution.py:23
  45.6 3.4 %collective-permute-start.14 = (f32[3,18,1,128]{3,2,1,0:T(1,128)S(1)}, f32[3,18,1,128]{3,2,1,0:T(1,128)S(1)}, u32[]{:S(2)}, u32[]{:S(2)}) collective-permute-start(f32[3,18,1,128]{3,2,1,0:T(1,128)S(1)} %get-tuple-element.15), channel_id=1, source_target_pairs={{2,0},{4,2},{6,4},{3,1},{5,3},{7,5},{10,8},{12,10},{14,12},{11,9},... | collective-permute-start | bytes 82952 | tf_op jit(solution)/shard_map/ppermute | solution.py:23
  48.9 1.3 %collective-permute-start.15 = (f32[3,18,1,128]{3,2,1,0:T(1,128)S(1)}, f32[3,18,1,128]{3,2,1,0:T(1,128)S(1)}, u32[]{:S(2)}, u32[]{:S(2)}) collective-permute-start(f32[3,18,1,128]{3,2,1,0:T(1,128)S(1)} %get-tuple-element.14), channel_id=1, source_target_pairs={{0,2},{2,4},{4,6},{1,3},{3,5},{5,7},{8,10},{10,12},{12,14},{9,11},... | collective-permute-start | bytes 82952 | tf_op jit(solution)/shard_map/ppermute | solution.py:22
  50.4 3.1 %collective-permute-done.15 = f32[3,18,1,128]{3,2,1,0:T(1,128)S(1)} collective-permute-done((f32[3,18,1,128]{3,2,1,0:T(1,128)S(1)}, f32[3,18,1,128]{3,2,1,0:T(1,128)S(1)}, u32[]{:S(2)}, u32[]{:S(2)}) %collective-permute-start.15) | collective-permute-done | bytes 27680 | tf_op jit(solution)/shard_map/ppermute | solution.py:22
  53.8 4.8 %collective-permute-start.16 = (f32[3,18,10,1]{3,2,1,0:T(8,128)S(1)}, f32[3,18,10,1]{3,2,1,0:T(8,128)S(1)}, u32[]{:S(2)}, u32[]{:S(2)}) collective-permute-start(f32[3,18,10,1]{3,2,1,0:T(8,128)S(1)} %get-tuple-element.7), channel_id=1, source_target_pairs={{1,0},{3,2},{5,4},{7,6},{9,8},{11,10},{13,12},{15,14},{17,16},{19,... | collective-permute-start | bytes 6488 | tf_op jit(solution)/shard_map/ppermute | solution.py:23
  60.0 2.3 %collective-permute-done.17 = f32[3,18,10,1]{3,2,1,0:T(8,128)S(1)} collective-permute-done((f32[3,18,10,1]{3,2,1,0:T(8,128)S(1)}, f32[3,18,10,1]{3,2,1,0:T(8,128)S(1)}, u32[]{:S(2)}, u32[]{:S(2)}) %collective-permute-start.17) | collective-permute-done | bytes 2192 | tf_op jit(solution)/shard_map/ppermute | solution.py:22
  63.2 2.2 %collective-permute-start.18 = (f32[3,1,8,128]{3,2,1,0:T(8,128)S(1)}, f32[3,1,8,128]{3,2,1,0:T(8,128)S(1)}, u32[]{:S(2)}, u32[]{:S(2)}) collective-permute-start(f32[3,1,8,128]{3,2,1,0:T(8,128)S(1)} %slice.706), channel_id=1, source_target_pairs={{8,0},{16,8},{24,16},{9,1},{17,9},{25,17},{10,2},{18,10},{26,18},{... | collective-permute-start | bytes 36872 | tf_op jit(solution)/shard_map/ppermute | solution.py:23
  65.6 2.1 %collective-permute-done.18 = f32[3,1,8,128]{3,2,1,0:T(8,128)S(1)} collective-permute-done((f32[3,1,8,128]{3,2,1,0:T(8,128)S(1)}, f32[3,1,8,128]{3,2,1,0:T(8,128)S(1)}, u32[]{:S(2)}, u32[]{:S(2)}) %collective-permute-start.18) | collective-permute-done | bytes 12320 | tf_op jit(solution)/shard_map/ppermute | solution.py:23
  67.7 1.9 %collective-permute-start.19 = (f32[3,1,8,128]{3,2,1,0:T(8,128)S(1)}, f32[3,1,8,128]{3,2,1,0:T(8,128)S(1)}, u32[]{:S(2)}, u32[]{:S(2)}) collective-permute-start(f32[3,1,8,128]{3,2,1,0:T(8,128)S(1)} %get-tuple-element.28), channel_id=1, source_target_pairs={{0,8},{8,16},{16,24},{1,9},{9,17},{17,25},{2,10},{10,18},{18,26},{... | collective-permute-start | bytes 36872 | tf_op jit(solution)/shard_map/ppermute | solution.py:22
  69.6 3.4 %collective-permute-done.19 = f32[3,1,8,128]{3,2,1,0:T(8,128)S(1)} collective-permute-done((f32[3,1,8,128]{3,2,1,0:T(8,128)S(1)}, f32[3,1,8,128]{3,2,1,0:T(8,128)S(1)}, u32[]{:S(2)}, u32[]{:S(2)}) %collective-permute-start.19) | collective-permute-done | bytes 12320 | tf_op jit(solution)/shard_map/ppermute | solution.py:22
  73.0 2.1 %collective-permute-start.20 = (f32[3,18,1,128]{3,2,1,0:T(1,128)S(1)}, f32[3,18,1,128]{3,2,1,0:T(1,128)S(1)}, u32[]{:S(2)}, u32[]{:S(2)}) collective-permute-start(f32[3,18,1,128]{3,2,1,0:T(1,128)S(1)} %get-tuple-element.13), channel_id=1, source_target_pairs={{2,0},{4,2},{6,4},{3,1},{5,3},{7,5},{10,8},{12,10},{14,12},{11,9},... | collective-permute-start | bytes 82952 | tf_op jit(solution)/shard_map/ppermute | solution.py:23
  76.5 3.2 %collective-permute-done.21 = f32[3,18,1,128]{3,2,1,0:T(1,128)S(1)} collective-permute-done((f32[3,18,1,128]{3,2,1,0:T(1,128)S(1)}, f32[3,18,1,128]{3,2,1,0:T(1,128)S(1)}, u32[]{:S(2)}, u32[]{:S(2)}) %collective-permute-start.21) | collective-permute-done | bytes 27680 | tf_op jit(solution)/shard_map/ppermute | solution.py:22
  80.0 5.8 %collective-permute-start.22 = (f32[3,18,10,1]{3,2,1,0:T(8,128)S(1)}, f32[3,18,10,1]{3,2,1,0:T(8,128)S(1)}, u32[]{:S(2)}, u32[]{:S(2)}) collective-permute-start(f32[3,18,10,1]{3,2,1,0:T(8,128)S(1)} %get-tuple-element.5), channel_id=1, source_target_pairs={{1,0},{3,2},{5,4},{7,6},{9,8},{11,10},{13,12},{15,14},{17,16},{19,... | collective-permute-start | bytes 6488 | tf_op jit(solution)/shard_map/ppermute | solution.py:23
  87.2 2.3 %collective-permute-done.23 = f32[3,18,10,1]{3,2,1,0:T(8,128)S(1)} collective-permute-done((f32[3,18,10,1]{3,2,1,0:T(8,128)S(1)}, f32[3,18,10,1]{3,2,1,0:T(8,128)S(1)}, u32[]{:S(2)}, u32[]{:S(2)}) %collective-permute-start.23) | collective-permute-done | bytes 2192 | tf_op jit(solution)/shard_map/ppermute | solution.py:22
  90.3 2.2 %collective-permute-start.24 = (f32[3,1,8,128]{3,2,1,0:T(8,128)S(1)}, f32[3,1,8,128]{3,2,1,0:T(8,128)S(1)}, u32[]{:S(2)}, u32[]{:S(2)}) collective-permute-start(f32[3,1,8,128]{3,2,1,0:T(8,128)S(1)} %slice.722), channel_id=1, source_target_pairs={{8,0},{16,8},{24,16},{9,1},{17,9},{25,17},{10,2},{18,10},{26,18},{... | collective-permute-start | bytes 36872 | tf_op jit(solution)/shard_map/ppermute | solution.py:23
  92.5 2.0 %all_gather.11 = f32[3,16,8,128]{3,2,1,0:T(8,128)S(1)} all-gather(f32[3,8,8,128]{3,2,1,0:T(8,128)S(1)} %multiply_add_fusion), channel_id=1, replica_groups=mesh['len'=4,'hgt'=4,'wid'=2] {'wid'}, dimensions={1}, use_global_device_ids=true | all-gather | bytes 294912 | tf_op jit(solution)/shard_map/all_gather | solution.py:91
  94.8 2.9 %collective-permute-start.25 = (f32[3,1,8,128]{3,2,1,0:T(8,128)S(1)}, f32[3,1,8,128]{3,2,1,0:T(8,128)S(1)}, u32[]{:S(2)}, u32[]{:S(2)}) collective-permute-start(f32[3,1,8,128]{3,2,1,0:T(8,128)S(1)} %get-tuple-element.21), channel_id=1, source_target_pairs={{0,8},{8,16},{16,24},{1,9},{9,17},{17,25},{2,10},{10,18},{18,26},{... | collective-permute-start | bytes 36872 | tf_op jit(solution)/shard_map/ppermute | solution.py:22
  97.7 2.4 %collective-permute-done.25 = f32[3,1,8,128]{3,2,1,0:T(8,128)S(1)} collective-permute-done((f32[3,1,8,128]{3,2,1,0:T(8,128)S(1)}, f32[3,1,8,128]{3,2,1,0:T(8,128)S(1)}, u32[]{:S(2)}, u32[]{:S(2)}) %collective-permute-start.25) | collective-permute-done | bytes 12320 | tf_op jit(solution)/shard_map/ppermute | solution.py:22
  100.1 1.6 %collective-permute-start.26 = (f32[3,18,1,128]{3,2,1,0:T(1,128)S(1)}, f32[3,18,1,128]{3,2,1,0:T(1,128)S(1)}, u32[]{:S(2)}, u32[]{:S(2)}) collective-permute-start(f32[3,18,1,128]{3,2,1,0:T(1,128)S(1)} %get-tuple-element.11), channel_id=1, source_target_pairs={{2,0},{4,2},{6,4},{3,1},{5,3},{7,5},{10,8},{12,10},{14,12},{11,9},... | collective-permute-start | bytes 82952 | tf_op jit(solution)/shard_map/ppermute | solution.py:23
  103.2 3.2 %collective-permute-done.27 = f32[3,18,1,128]{3,2,1,0:T(1,128)S(1)} collective-permute-done((f32[3,18,1,128]{3,2,1,0:T(1,128)S(1)}, f32[3,18,1,128]{3,2,1,0:T(1,128)S(1)}, u32[]{:S(2)}, u32[]{:S(2)}) %collective-permute-start.27) | collective-permute-done | bytes 27680 | tf_op jit(solution)/shard_map/ppermute | solution.py:22
  106.7 5.8 %collective-permute-start.28 = (f32[3,18,10,1]{3,2,1,0:T(8,128)S(1)}, f32[3,18,10,1]{3,2,1,0:T(8,128)S(1)}, u32[]{:S(2)}, u32[]{:S(2)}) collective-permute-start(f32[3,18,10,1]{3,2,1,0:T(8,128)S(1)} %get-tuple-element.3), channel_id=1, source_target_pairs={{1,0},{3,2},{5,4},{7,6},{9,8},{11,10},{13,12},{15,14},{17,16},{19,... | collective-permute-start | bytes 6488 | tf_op jit(solution)/shard_map/ppermute | solution.py:23
  113.9 2.3 %collective-permute-done.29 = f32[3,18,10,1]{3,2,1,0:T(8,128)S(1)} collective-permute-done((f32[3,18,10,1]{3,2,1,0:T(8,128)S(1)}, f32[3,18,10,1]{3,2,1,0:T(8,128)S(1)}, u32[]{:S(2)}, u32[]{:S(2)}) %collective-permute-start.29) | collective-permute-done | bytes 2192 | tf_op jit(solution)/shard_map/ppermute | solution.py:22
  (117 shorter events, 24.0 us)
Async XLA Ops:
  1.7 16.8 %collective-permute-start.2 = (f32[3,16,1,128]{3,2,1,0:T(1,128)S(1)}, f32[3,16,1,128]{3,2,1,0:T(1,128)S(1)}, u32[]{:S(2)}, u32[]{:S(2)}) collective-permute-start(f32[3,16,1,128]{3,2,1,0:T(1,128)S(1)} %get-tuple-element.57), channel_id=1, source_target_pairs={{0,2},{2,4},{4,6},{1,3},{3,5},{5,7},{8,10},{10,12},{12,14},{9,11},... | collective-permute-start | bytes 73736 | tf_op jit(solution)/shard_map/ppermute | solution.py:22
  3.0 15.5 %collective-permute-start.3 = (f32[3,16,1,128]{3,2,1,0:T(1,128)S(1)}, f32[3,16,1,128]{3,2,1,0:T(1,128)S(1)}, u32[]{:S(2)}, u32[]{:S(2)}) collective-permute-start(f32[3,16,1,128]{3,2,1,0:T(1,128)S(1)} %get-tuple-element.56), channel_id=1, source_target_pairs={{2,0},{4,2},{6,4},{3,1},{5,3},{7,5},{10,8},{12,10},{14,12},{11,9},... | collective-permute-start | bytes 73736 | tf_op jit(solution)/shard_map/ppermute | solution.py:23
  7.7 6.5 %collective-permute-start = (f32[3,1,8,128]{3,2,1,0:T(8,128)S(1)}, f32[3,1,8,128]{3,2,1,0:T(8,128)S(1)}, u32[]{:S(2)}, u32[]{:S(2)}) collective-permute-start(f32[3,1,8,128]{3,2,1,0:T(8,128)S(1)} %get-tuple-element.55), channel_id=1, source_target_pairs={{0,8},{8,16},{16,24},{24,0},{1,9},{9,17},{17,25},{25,1},{2,10},{10... | collective-permute-start | bytes 36872 | tf_op jit(solution)/shard_map/ppermute | solution.py:22
  8.9 5.3 %collective-permute-start.1 = (f32[3,1,8,128]{3,2,1,0:T(8,128)S(1)}, f32[3,1,8,128]{3,2,1,0:T(8,128)S(1)}, u32[]{:S(2)}, u32[]{:S(2)}) collective-permute-start(f32[3,1,8,128]{3,2,1,0:T(8,128)S(1)} %get-tuple-element.54), channel_id=1, source_target_pairs={{8,0},{16,8},{24,16},{0,24},{9,1},{17,9},{25,17},{1,25},{10,2},{18... | collective-permute-start | bytes 36872 | tf_op jit(solution)/shard_map/ppermute | solution.py:23
  10.8 4.4 %collective-permute-start.12 = (f32[3,1,8,128]{3,2,1,0:T(8,128)S(1)}, f32[3,1,8,128]{3,2,1,0:T(8,128)S(1)}, u32[]{:S(2)}, u32[]{:S(2)}) collective-permute-start(f32[3,1,8,128]{3,2,1,0:T(8,128)S(1)} %slice.574), channel_id=1, source_target_pairs={{8,0},{16,8},{24,16},{9,1},{17,9},{25,17},{10,2},{18,10},{26,18},{... | collective-permute-start | bytes 36872 | tf_op jit(solution)/shard_map/ppermute | solution.py:23
  13.0 1.0 copy-start.2
  13.0 1.0 copy-start
  15.2 29.5 %collective-permute-start.13 = (f32[3,1,8,128]{3,2,1,0:T(8,128)S(1)}, f32[3,1,8,128]{3,2,1,0:T(8,128)S(1)}, u32[]{:S(2)}, u32[]{:S(2)}) collective-permute-start(f32[3,1,8,128]{3,2,1,0:T(8,128)S(1)} %get-tuple-element.35), channel_id=1, source_target_pairs={{0,8},{8,16},{16,24},{1,9},{9,17},{17,25},{2,10},{10,18},{18,26},{... | collective-permute-start | bytes 36872 | tf_op jit(solution)/shard_map/ppermute | solution.py:22
  22.8 7.7 %collective-permute-start.4 = (f32[3,1,8,128]{3,2,1,0:T(8,128)S(1)}, f32[3,1,8,128]{3,2,1,0:T(8,128)S(1)}, u32[]{:S(2)}, u32[]{:S(2)}) collective-permute-start(f32[3,1,8,128]{3,2,1,0:T(8,128)S(1)} %get-tuple-element.48), channel_id=1, source_target_pairs={{0,8},{8,16},{16,24},{24,0},{1,9},{9,17},{17,25},{25,1},{2,10},{10... | collective-permute-start | bytes 36872 | tf_op jit(solution)/shard_map/ppermute | solution.py:22
  22.9 7.7 %collective-permute-start.5 = (f32[3,1,8,128]{3,2,1,0:T(8,128)S(1)}, f32[3,1,8,128]{3,2,1,0:T(8,128)S(1)}, u32[]{:S(2)}, u32[]{:S(2)}) collective-permute-start(f32[3,1,8,128]{3,2,1,0:T(8,128)S(1)} %get-tuple-element.47), channel_id=1, source_target_pairs={{8,0},{16,8},{24,16},{0,24},{9,1},{17,9},{25,17},{1,25},{10,2},{18... | collective-permute-start | bytes 36872 | tf_op jit(solution)/shard_map/ppermute | solution.py:23
  25.3 5.6 %collective-permute-start.6 = (f32[3,16,1,128]{3,2,1,0:T(1,128)S(1)}, f32[3,16,1,128]{3,2,1,0:T(1,128)S(1)}, u32[]{:S(2)}, u32[]{:S(2)}) collective-permute-start(f32[3,16,1,128]{3,2,1,0:T(1,128)S(1)} %get-tuple-element.50), channel_id=1, source_target_pairs={{0,2},{2,4},{4,6},{1,3},{3,5},{5,7},{8,10},{10,12},{12,14},{9,11},... | collective-permute-start | bytes 73736 | tf_op jit(solution)/shard_map/ppermute | solution.py:22
  26.6 4.9 %collective-permute-start.7 = (f32[3,16,1,128]{3,2,1,0:T(1,128)S(1)}, f32[3,16,1,128]{3,2,1,0:T(1,128)S(1)}, u32[]{:S(2)}, u32[]{:S(2)}) collective-permute-start(f32[3,16,1,128]{3,2,1,0:T(1,128)S(1)} %get-tuple-element.49), channel_id=1, source_target_pairs={{2,0},{4,2},{6,4},{3,1},{5,3},{7,5},{10,8},{12,10},{14,12},{11,9},... | collective-permute-start | bytes 73736 | tf_op jit(solution)/shard_map/ppermute | solution.py:23
  35.6 8.3 %collective-permute-start.8 = (f32[3,1,8,128]{3,2,1,0:T(8,128)S(1)}, f32[3,1,8,128]{3,2,1,0:T(8,128)S(1)}, u32[]{:S(2)}, u32[]{:S(2)}) collective-permute-start(f32[3,1,8,128]{3,2,1,0:T(8,128)S(1)} %get-tuple-element.41), channel_id=1, source_target_pairs={{0,8},{8,16},{16,24},{24,0},{1,9},{9,17},{17,25},{25,1},{2,10},{10... | collective-permute-start | bytes 36872 | tf_op jit(solution)/shard_map/ppermute | solution.py:22
  35.7 14.6 %collective-permute-start.9 = (f32[3,1,8,128]{3,2,1,0:T(8,128)S(1)}, f32[3,1,8,128]{3,2,1,0:T(8,128)S(1)}, u32[]{:S(2)}, u32[]{:S(2)}) collective-permute-start(f32[3,1,8,128]{3,2,1,0:T(8,128)S(1)} %get-tuple-element.40), channel_id=1, source_target_pairs={{8,0},{16,8},{24,16},{0,24},{9,1},{17,9},{25,17},{1,25},{10,2},{18... | collective-permute-start | bytes 36872 | tf_op jit(solution)/shard_map/ppermute | solution.py:23
  38.1 12.2 %collective-permute-start.10 = (f32[3,16,1,128]{3,2,1,0:T(1,128)S(1)}, f32[3,16,1,128]{3,2,1,0:T(1,128)S(1)}, u32[]{:S(2)}, u32[]{:S(2)}) collective-permute-start(f32[3,16,1,128]{3,2,1,0:T(1,128)S(1)} %get-tuple-element.43), channel_id=1, source_target_pairs={{0,2},{2,4},{4,6},{1,3},{3,5},{5,7},{8,10},{10,12},{12,14},{9,11},... | collective-permute-start | bytes 73736 | tf_op jit(solution)/shard_map/ppermute | solution.py:22
  39.4 11.0 %collective-permute-start.11 = (f32[3,16,1,128]{3,2,1,0:T(1,128)S(1)}, f32[3,16,1,128]{3,2,1,0:T(1,128)S(1)}, u32[]{:S(2)}, u32[]{:S(2)}) collective-permute-start(f32[3,16,1,128]{3,2,1,0:T(1,128)S(1)} %get-tuple-element.42), channel_id=1, source_target_pairs={{2,0},{4,2},{6,4},{3,1},{5,3},{7,5},{10,8},{12,10},{14,12},{11,9},... | collective-permute-start | bytes 73736 | tf_op jit(solution)/shard_map/ppermute | solution.py:23
  45.6 4.8 %collective-permute-start.14 = (f32[3,18,1,128]{3,2,1,0:T(1,128)S(1)}, f32[3,18,1,128]{3,2,1,0:T(1,128)S(1)}, u32[]{:S(2)}, u32[]{:S(2)}) collective-permute-start(f32[3,18,1,128]{3,2,1,0:T(1,128)S(1)} %get-tuple-element.15), channel_id=1, source_target_pairs={{2,0},{4,2},{6,4},{3,1},{5,3},{7,5},{10,8},{12,10},{14,12},{11,9},... | collective-permute-start | bytes 82952 | tf_op jit(solution)/shard_map/ppermute | solution.py:23
  48.9 4.6 %collective-permute-start.15 = (f32[3,18,1,128]{3,2,1,0:T(1,128)S(1)}, f32[3,18,1,128]{3,2,1,0:T(1,128)S(1)}, u32[]{:S(2)}, u32[]{:S(2)}) collective-permute-start(f32[3,18,1,128]{3,2,1,0:T(1,128)S(1)} %get-tuple-element.14), channel_id=1, source_target_pairs={{0,2},{2,4},{4,6},{1,3},{3,5},{5,7},{8,10},{10,12},{12,14},{9,11},... | collective-permute-start | bytes 82952 | tf_op jit(solution)/shard_map/ppermute | solution.py:22
  53.8 6.2 %collective-permute-start.16 = (f32[3,18,10,1]{3,2,1,0:T(8,128)S(1)}, f32[3,18,10,1]{3,2,1,0:T(8,128)S(1)}, u32[]{:S(2)}, u32[]{:S(2)}) collective-permute-start(f32[3,18,10,1]{3,2,1,0:T(8,128)S(1)} %get-tuple-element.7), channel_id=1, source_target_pairs={{1,0},{3,2},{5,4},{7,6},{9,8},{11,10},{13,12},{15,14},{17,16},{19,... | collective-permute-start | bytes 6488 | tf_op jit(solution)/shard_map/ppermute | solution.py:23
  58.7 3.7 %collective-permute-start.17 = (f32[3,18,10,1]{3,2,1,0:T(8,128)S(1)}, f32[3,18,10,1]{3,2,1,0:T(8,128)S(1)}, u32[]{:S(2)}, u32[]{:S(2)}) collective-permute-start(f32[3,18,10,1]{3,2,1,0:T(8,128)S(1)} %get-tuple-element.6), channel_id=1, source_target_pairs={{0,1},{2,3},{4,5},{6,7},{8,9},{10,11},{12,13},{14,15},{16,17},{18,... | collective-permute-start | bytes 6488 | tf_op jit(solution)/shard_map/ppermute | solution.py:22
  63.2 4.4 %collective-permute-start.18 = (f32[3,1,8,128]{3,2,1,0:T(8,128)S(1)}, f32[3,1,8,128]{3,2,1,0:T(8,128)S(1)}, u32[]{:S(2)}, u32[]{:S(2)}) collective-permute-start(f32[3,1,8,128]{3,2,1,0:T(8,128)S(1)} %slice.706), channel_id=1, source_target_pairs={{8,0},{16,8},{24,16},{9,1},{17,9},{25,17},{10,2},{18,10},{26,18},{... | collective-permute-start | bytes 36872 | tf_op jit(solution)/shard_map/ppermute | solution.py:23
  67.7 5.3 %collective-permute-start.19 = (f32[3,1,8,128]{3,2,1,0:T(8,128)S(1)}, f32[3,1,8,128]{3,2,1,0:T(8,128)S(1)}, u32[]{:S(2)}, u32[]{:S(2)}) collective-permute-start(f32[3,1,8,128]{3,2,1,0:T(8,128)S(1)} %get-tuple-element.28), channel_id=1, source_target_pairs={{0,8},{8,16},{16,24},{1,9},{9,17},{17,25},{2,10},{10,18},{18,26},{... | collective-permute-start | bytes 36872 | tf_op jit(solution)/shard_map/ppermute | solution.py:22
  73.0 3.5 %collective-permute-start.20 = (f32[3,18,1,128]{3,2,1,0:T(1,128)S(1)}, f32[3,18,1,128]{3,2,1,0:T(1,128)S(1)}, u32[]{:S(2)}, u32[]{:S(2)}) collective-permute-start(f32[3,18,1,128]{3,2,1,0:T(1,128)S(1)} %get-tuple-element.13), channel_id=1, source_target_pairs={{2,0},{4,2},{6,4},{3,1},{5,3},{7,5},{10,8},{12,10},{14,12},{11,9},... | collective-permute-start | bytes 82952 | tf_op jit(solution)/shard_map/ppermute | solution.py:23
  75.1 4.6 %collective-permute-start.21 = (f32[3,18,1,128]{3,2,1,0:T(1,128)S(1)}, f32[3,18,1,128]{3,2,1,0:T(1,128)S(1)}, u32[]{:S(2)}, u32[]{:S(2)}) collective-permute-start(f32[3,18,1,128]{3,2,1,0:T(1,128)S(1)} %get-tuple-element.12), channel_id=1, source_target_pairs={{0,2},{2,4},{4,6},{1,3},{3,5},{5,7},{8,10},{10,12},{12,14},{9,11},... | collective-permute-start | bytes 82952 | tf_op jit(solution)/shard_map/ppermute | solution.py:22
  80.0 7.2 %collective-permute-start.22 = (f32[3,18,10,1]{3,2,1,0:T(8,128)S(1)}, f32[3,18,10,1]{3,2,1,0:T(8,128)S(1)}, u32[]{:S(2)}, u32[]{:S(2)}) collective-permute-start(f32[3,18,10,1]{3,2,1,0:T(8,128)S(1)} %get-tuple-element.5), channel_id=1, source_target_pairs={{1,0},{3,2},{5,4},{7,6},{9,8},{11,10},{13,12},{15,14},{17,16},{19,... | collective-permute-start | bytes 6488 | tf_op jit(solution)/shard_map/ppermute | solution.py:23
  85.8 3.7 %collective-permute-start.23 = (f32[3,18,10,1]{3,2,1,0:T(8,128)S(1)}, f32[3,18,10,1]{3,2,1,0:T(8,128)S(1)}, u32[]{:S(2)}, u32[]{:S(2)}) collective-permute-start(f32[3,18,10,1]{3,2,1,0:T(8,128)S(1)} %get-tuple-element.4), channel_id=1, source_target_pairs={{0,1},{2,3},{4,5},{6,7},{8,9},{10,11},{12,13},{14,15},{16,17},{18,... | collective-permute-start | bytes 6488 | tf_op jit(solution)/shard_map/ppermute | solution.py:22
  90.3 4.4 %collective-permute-start.24 = (f32[3,1,8,128]{3,2,1,0:T(8,128)S(1)}, f32[3,1,8,128]{3,2,1,0:T(8,128)S(1)}, u32[]{:S(2)}, u32[]{:S(2)}) collective-permute-start(f32[3,1,8,128]{3,2,1,0:T(8,128)S(1)} %slice.722), channel_id=1, source_target_pairs={{8,0},{16,8},{24,16},{9,1},{17,9},{25,17},{10,2},{18,10},{26,18},{... | collective-permute-start | bytes 36872 | tf_op jit(solution)/shard_map/ppermute | solution.py:23
  94.8 5.3 %collective-permute-start.25 = (f32[3,1,8,128]{3,2,1,0:T(8,128)S(1)}, f32[3,1,8,128]{3,2,1,0:T(8,128)S(1)}, u32[]{:S(2)}, u32[]{:S(2)}) collective-permute-start(f32[3,1,8,128]{3,2,1,0:T(8,128)S(1)} %get-tuple-element.21), channel_id=1, source_target_pairs={{0,8},{8,16},{16,24},{1,9},{9,17},{17,25},{2,10},{10,18},{18,26},{... | collective-permute-start | bytes 36872 | tf_op jit(solution)/shard_map/ppermute | solution.py:22
  100.1 3.0 %collective-permute-start.26 = (f32[3,18,1,128]{3,2,1,0:T(1,128)S(1)}, f32[3,18,1,128]{3,2,1,0:T(1,128)S(1)}, u32[]{:S(2)}, u32[]{:S(2)}) collective-permute-start(f32[3,18,1,128]{3,2,1,0:T(1,128)S(1)} %get-tuple-element.11), channel_id=1, source_target_pairs={{2,0},{4,2},{6,4},{3,1},{5,3},{7,5},{10,8},{12,10},{14,12},{11,9},... | collective-permute-start | bytes 82952 | tf_op jit(solution)/shard_map/ppermute | solution.py:23
  101.8 4.6 %collective-permute-start.27 = (f32[3,18,1,128]{3,2,1,0:T(1,128)S(1)}, f32[3,18,1,128]{3,2,1,0:T(1,128)S(1)}, u32[]{:S(2)}, u32[]{:S(2)}) collective-permute-start(f32[3,18,1,128]{3,2,1,0:T(1,128)S(1)} %get-tuple-element.10), channel_id=1, source_target_pairs={{0,2},{2,4},{4,6},{1,3},{3,5},{5,7},{8,10},{10,12},{12,14},{9,11},... | collective-permute-start | bytes 82952 | tf_op jit(solution)/shard_map/ppermute | solution.py:22
  106.7 7.2 %collective-permute-start.28 = (f32[3,18,10,1]{3,2,1,0:T(8,128)S(1)}, f32[3,18,10,1]{3,2,1,0:T(8,128)S(1)}, u32[]{:S(2)}, u32[]{:S(2)}) collective-permute-start(f32[3,18,10,1]{3,2,1,0:T(8,128)S(1)} %get-tuple-element.3), channel_id=1, source_target_pairs={{1,0},{3,2},{5,4},{7,6},{9,8},{11,10},{13,12},{15,14},{17,16},{19,... | collective-permute-start | bytes 6488 | tf_op jit(solution)/shard_map/ppermute | solution.py:23
  112.5 3.7 %collective-permute-start.29 = (f32[3,18,10,1]{3,2,1,0:T(8,128)S(1)}, f32[3,18,10,1]{3,2,1,0:T(8,128)S(1)}, u32[]{:S(2)}, u32[]{:S(2)}) collective-permute-start(f32[3,18,10,1]{3,2,1,0:T(8,128)S(1)} %get-tuple-element.2), channel_id=1, source_target_pairs={{0,1},{2,3},{4,5},{6,7},{8,9},{10,11},{12,13},{14,15},{16,17},{18,... | collective-permute-start | bytes 6488 | tf_op jit(solution)/shard_map/ppermute | solution.py:22
  (3 other events, 2.4 us)
where the time goes:
time: 119 us; the launch traced here: 118 us
  starting transfers between devices  69.3 us (58%)
  waiting for transfers between devices  26 us (22%)
  blocking collectives  9.61 us (8%)
  other arithmetic  6.99 us (6%)
  local copies, waits for them, and re-layouts  5.1 us (4%)
  between operations  1.3 us (1%)
    ppermute x15, starting transfers between devices, padded_2(): after = lax.ppermute(leading, axis, down)  48.5 us
    ppermute x15, waiting for transfers between devices, padded_2(): before = lax.ppermute(last, axis, up)  22.3 us
    ppermute x15, starting transfers between devices, padded_2(): before = lax.ppermute(last, axis, up)  20.8 us
    all_gather x3, blocking collectives, on_device(): precursor = lax.all_gather(own_rows, 'wid', axis=1, tiled=True)  9.61 us
    ppermute x15, waiting for transfers between devices, padded_2(): after = lax.ppermute(leading, axis, down)  3.79 us
    slice x9, local copies, waits for them, and re-layouts, padded_2(): leading = lax.slice_in_dim(x, 0, width, axis=dim)  2.58 us
  transfers between devices with their start and end apart: 30, of which 12 were waited for; matrix products, arithmetic and copies ran while one was open for 4% of the time, Pallas kernels for 0%

commit v1 on v0

v1 whole, which is shorter than its diff:
```python
import functools

import jax
import jax.numpy as jnp
from jax import lax
from jax.experimental import pallas as pl
from jax.experimental.pallas import tpu as pltpu
from jax.sharding import PartitionSpec as P

STEPS = 3
UNROLL = 2

time_step = 0.3
viscosity = 0.04
smag_coef = 0.03
spread_eps = 1e-05


def stencil(u, len_dn, len_up, hgt_dn, hgt_up, wid_dn, wid_up):
    dn, up = (len_dn, hgt_dn, wid_dn), (len_up, hgt_up, wid_up)
    diff = [[up[d][c] - dn[d][c] for d in range(3)] for c in range(3)]
    diag = diff[0][0] * diff[0][0] + diff[1][1] * diff[1][1] + diff[2][2] * diff[2][2]
    s01 = diff[0][1] + diff[1][0]
    s02 = diff[0][2] + diff[2][0]
    s12 = diff[1][2] + diff[2][1]
    total = 2.0 * diag + s01 * s01 + s02 * s02 + s12 * s12
    nu = time_step * viscosity + (0.5 * time_step * smag_coef) * jnp.sqrt(total)
    half = [(0.5 * time_step) * u[d] for d in range(3)]
    out = []
    for c in range(3):
        lap = (up[0][c] + dn[0][c]) + (up[1][c] + dn[1][c]) + (up[2][c] + dn[2][c]) - 6.0 * u[c]
        adv = half[0] * diff[c][0] + half[1] * diff[c][1] + half[2] * diff[c][2]
        out.append(u[c] + nu * lap - adv)
    return out


def kernel(counts, pre_ref, face_ref, solid_ref, prof_ref, spread_ref, pre_out, face_out,
           state, hsend, hrecv, wsend, wrecv, load_sem, send_sem, recv_sem):
    n_len, n_hgt, n_wid = counts
    planes, rows, cols = solid_ref.shape
    me_len, me_hgt, me_wid = lax.axis_index("len"), lax.axis_index("hgt"), lax.axis_index("wid")
    next_len = lax.rem(me_len + 1, n_len)
    prev_len = lax.rem(me_len + n_len - 1, n_len)

    partners = (
        ("len", next_len, None),
        ("len", prev_len, None),
        ("hgt", me_hgt + 1, me_hgt < n_hgt - 1),
        ("hgt", me_hgt - 1, me_hgt > 0),
        ("wid", me_wid + 1, me_wid < n_wid - 1),
        ("wid", me_wid - 1, me_wid > 0),
    )

    def guarded(cond, fn):
        if cond is None:
            fn()
        else:
            pl.when(cond)(fn)

    loads = [
        pltpu.make_async_copy(pre_ref, state.at[0, 0:3, 1:planes + 1], load_sem.at[0]),
        pltpu.make_async_copy(face_ref, state.at[0, 3:6, 1:planes + 1], load_sem.at[1]),
    ]
    for copy in loads:
        copy.start()

    barrier = pltpu.get_barrier_semaphore()
    for axis, target, cond in partners:
        guarded(cond, lambda axis=axis, target=target: pl.semaphore_signal(
            barrier, inc=1, device_id={axis: target}, device_id_type=pl.DeviceIdType.MESH))

    sub = lax.broadcasted_iota(jnp.int32, (rows, cols), 0)
    lane = lax.broadcasted_iota(jnp.int32, (rows, cols), 1)

    zero_rows = jnp.zeros(hrecv.shape[2:], jnp.float32)
    zero_cols = jnp.zeros(wrecv.shape[2:], jnp.float32)

    def zero(ref, side, value):
        def go():
            for s in range(STEPS):
                ref[s, side] = value
        return go

    pl.when(me_hgt == 0)(zero(hrecv, 0, zero_rows))
    pl.when(me_hgt == n_hgt - 1)(zero(hrecv, 1, zero_rows))
    pl.when(me_wid == 0)(zero(wrecv, 0, zero_cols))
    pl.when(me_wid == n_wid - 1)(zero(wrecv, 1, zero_cols))

    pick = lax.broadcasted_iota(jnp.int32, (rows, rows), 0) == lax.broadcasted_iota(jnp.int32, (rows, rows), 1)

    def column(ref, c):
        return jnp.sum(jnp.where(pick, jnp.broadcast_to(ref[c:c + 1, :], (rows, rows)), 0.0), axis=1, keepdims=True)

    profile = [column(prof_ref, c) for c in range(3)]
    target_spread = [column(spread_ref, c) for c in range(3)]

    def copies(s):
        srcs = [state.at[s, :, planes], state.at[s, :, 1], hsend.at[s, 1], hsend.at[s, 0], wsend.at[s], wsend.at[s]]
        dsts = [state.at[s, :, 0], state.at[s, :, planes + 1], hrecv.at[s, 0], hrecv.at[s, 1], wrecv.at[s, 0], wrecv.at[s, 1]]
        return [
            pltpu.make_async_remote_copy(
                src_ref=srcs[k], dst_ref=dsts[k], send_sem=send_sem.at[s, k], recv_sem=recv_sem.at[s, k],
                device_id={partners[k][0]: partners[k][1]}, device_id_type=pl.DeviceIdType.MESH)
            for k in range(6)
        ]

    def pack(s, l, pre, face, acc):
        for c, x in enumerate(list(pre) + list(face)):
            hsend[s, 0, c, pl.ds(l, 1), :] = x[0:1]
            hsend[s, 1, c, pl.ds(l, 1), :] = x[rows - 1:rows]
        mine = (lane >> 1) == l
        return [jnp.where(mine, pltpu.roll(face[c], 2 * l + 1, 1), acc[c]) for c in range(3)]

    for copy in loads:
        copy.wait()
    no_acc = [jnp.zeros((rows, cols), jnp.float32)] * 3

    def first(l, acc):
        x = [state[0, c, l + 1] for c in range(6)]
        return pack(0, l, x[:3], x[3:], acc)

    acc = lax.fori_loop(0, planes, first, no_acc, unroll=UNROLL)
    for c in range(3):
        wsend[0, c] = acc[c]

    expected = sum([jnp.int32(1) if cond is None else cond.astype(jnp.int32) for _, _, cond in partners])
    pl.semaphore_wait(barrier, expected)

    arrives = (None, None, me_hgt > 0, me_hgt < n_hgt - 1, me_wid > 0, me_wid < n_wid - 1)
    even = (lane & 1) == 0
    for s in range(STEPS):
        sends = copies(s)
        for k in range(6):
            guarded(partners[k][2], sends[k].start)
        for k in range(6):
            guarded(arrives[k], sends[k].wait_recv)
        for c in range(3):
            recycled = state[s, c, 0]
            mean = jnp.sum(recycled, axis=1, keepdims=True) * (1.0 / cols)
            fluct = recycled - mean
            var = jnp.sum(fluct * fluct, axis=1, keepdims=True) * (1.0 / cols)
            inlet = profile[c] + target_spread[c] / jnp.sqrt(var + spread_eps) * fluct
            state[s, 3 + c, 0] = jnp.where(me_len == 0, inlet, state[s, 3 + c, 0])
            state[s, 3 + c, planes + 1] = jnp.where(
                me_len == n_len - 1, state[s, 3 + c, planes], state[s, 3 + c, planes + 1])
        ghosts = [
            jnp.where(even, pltpu.roll(wrecv[s, 1, c], cols - 1, 1), pltpu.roll(wrecv[s, 0, c], 1, 1))
            for c in range(3)
        ]

        def plane(l, acc, s=s, ghosts=ghosts):
            def zone(z):
                u = [state[s, 3 * z + c, l + 1] for c in range(3)]
                len_dn = [state[s, 3 * z + c, l] for c in range(3)]
                len_up = [state[s, 3 * z + c, l + 2] for c in range(3)]
                hgt_dn = [jnp.where(sub == 0, hrecv[s, 0, 3 * z + c, pl.ds(l, 1), :], pltpu.roll(u[c], 1, 0)) for c in range(3)]
                hgt_up = [jnp.where(sub == rows - 1, hrecv[s, 1, 3 * z + c, pl.ds(l, 1), :], pltpu.roll(u[c], rows - 1, 0)) for c in range(3)]
                if z == 0:
                    edge = [0.0] * 3
                else:
                    edge = [pltpu.roll(ghosts[c], cols - (2 * l + 1), 1) for c in range(3)]
                wid_dn = [jnp.where(lane == 0, edge[c], pltpu.roll(u[c], 1, 1)) for c in range(3)]
                wid_up = [jnp.where(lane == cols - 1, edge[c], pltpu.roll(u[c], cols - 1, 1)) for c in range(3)]
                return stencil(u, len_dn, len_up, hgt_dn, hgt_up, wid_dn, wid_up)

            pre = zone(0)
            share = (1 - solid_ref[l]).astype(jnp.float32)
            face = [x * share for x in zone(1)]
            if s == STEPS - 1:
                for c in range(3):
                    pre_out[c, l] = pre[c]
                    face_out[c, l] = face[c]
                return acc
            for c in range(3):
                state[s + 1, c, l + 1] = pre[c]
                state[s + 1, 3 + c, l + 1] = face[c]
            return pack(s + 1, l, pre, face, acc)

        acc = lax.fori_loop(0, planes, plane, no_acc, unroll=UNROLL)
        if s < STEPS - 1:
            for c in range(3):
                wsend[s + 1, c] = acc[c]

    for s in range(STEPS):
        sends = copies(s)
        for k in range(6):
            guarded(partners[k][2], sends[k].wait_send)


def on_device(counts, precursor, face, solid, inlet_profile, target_spread):
    planes, rows, cols = solid.shape
    vmem = pl.BlockSpec(memory_space=pltpu.VMEM)
    hbm = pl.BlockSpec(memory_space=pl.ANY)
    f32 = jnp.float32
    return pl.pallas_call(
        functools.partial(kernel, counts),
        out_shape=(jax.ShapeDtypeStruct(precursor.shape, f32), jax.ShapeDtypeStruct(face.shape, f32)),
        in_specs=[hbm, hbm, vmem, vmem, vmem],
        out_specs=(vmem, vmem),
        scratch_shapes=[
            pltpu.VMEM((STEPS, 6, planes + 2, rows, cols), f32),
            pltpu.VMEM((STEPS, 2, 6, planes, cols), f32),
            pltpu.VMEM((STEPS, 2, 6, planes, cols), f32),
            pltpu.VMEM((STEPS, 3, rows, cols), f32),
            pltpu.VMEM((STEPS, 2, 3, rows, cols), f32),
            pltpu.SemaphoreType.DMA((2,)),
            pltpu.SemaphoreType.DMA((STEPS, 6)),
            pltpu.SemaphoreType.DMA((STEPS, 6)),
        ],
        compiler_params=pltpu.CompilerParams(
            collective_id=0, has_side_effects=True, vmem_limit_bytes=16 * 1024 * 1024),
    )(precursor, face, solid, inlet_profile, target_spread)


def solution(mesh):
    counts = (mesh.shape["len"], mesh.shape["hgt"], mesh.shape["wid"])
    return jax.shard_map(
        functools.partial(on_device, counts),
        mesh=mesh,
        in_specs=(
            P(None, "len", "hgt", None),
            P(None, "len", "hgt", "wid"),
            P("len", "hgt", "wid"),
            P(None, "hgt"),
            P(None, "hgt"),
        ),
        out_specs=(P(None, "len", "hgt", None), P(None, "len", "hgt", "wid")),
        check_vma=False,
    )
```

time: 119 us -> 26.1 us (0.22)
  the two profiles are of different devices: /device:TPU:29 before, /device:TPU:0 now
where the time goes in v1:
time: 26.1 us; the launch traced here: 25.8 us
  Pallas kernels  19.8 us (76%)
  local copies, waits for them, and re-layouts  5.4 us (21%)
  between operations  0.65 us (2%)
    pallas_call x1, Pallas kernels, on_device(): pl.pallas_call(functools.partial(kernel, counts), out_shape=(jax.ShapeDty...  19.8 us
    unnamed x12, local copies, waits for them, and re-layouts  5.4 us

profile of v1, /device:TPU:0, one launch (start us, length us, event | category | flops | bytes accessed | tf_op | source)
XLA Modules:
  0.0 25.8 jit_solution(3903723298873614275)
XLA Ops:
  0.6 0.0 copy-start
  0.6 0.9 %copy-done = f32[3,16,8,128]{3,2,1,0:T(8,128)S(1)} copy-done((f32[3,16,8,128]{3,2,1,0:T(8,128)S(1)}, f32[3,16,8,128]{3,2,1,0:T(8,128)}, u32[]{:S(2)}) %copy-start) | copy-done | bytes 196632
  1.6 0.0 copy-start.1
  1.6 0.9 %copy-done.1 = f32[3,16,8,128]{3,2,1,0:T(8,128)S(1)} copy-done((f32[3,16,8,128]{3,2,1,0:T(8,128)S(1)}, f32[3,16,8,128]{3,2,1,0:T(8,128)}, u32[]{:S(2)}) %copy-start.1) | copy-done | bytes 196632
  2.5 0.0 copy-start.2
  2.5 0.8 %copy-done.2 = s32[16,8,128]{2,1,0:T(8,128)S(1)} copy-done((s32[16,8,128]{2,1,0:T(8,128)S(1)}, s32[16,8,128]{2,1,0:T(8,128)}, u32[]{:S(2)}) %copy-start.2) | copy-done | bytes 65560
  3.3 0.0 copy-start.3
  3.3 0.7 %copy-done.3 = f32[3,8]{1,0:T(4,128)S(1)} copy-done((f32[3,8]{1,0:T(4,128)S(1)}, f32[3,8]{1,0:T(4,128)}, u32[]{:S(2)}) %copy-start.3) | copy-done | bytes 120
  4.0 0.0 copy-start.4
  4.0 0.7 %copy-done.4 = f32[3,8]{1,0:T(4,128)S(1)} copy-done((f32[3,8]{1,0:T(4,128)S(1)}, f32[3,8]{1,0:T(4,128)}, u32[]{:S(2)}) %copy-start.4) | copy-done | bytes 120
  4.7 19.8 %shard_map.68 = (f32[3,16,8,128]{3,2,1,0:T(8,128)S(1)}, f32[3,16,8,128]{3,2,1,0:T(8,128)S(1)}) custom-call(f32[3,16,8,128]{3,2,1,0:T(8,128)S(1)} %copy-done, f32[3,16,8,128]{3,2,1,0:T(8,128)S(1)} %copy-done.1, s32[16,8,128]{2,1,0:T(8,128)S(1)} %copy-done.2, f32[3,8]{1,0:T(4,128)S(1)} %copy-done.3, f32[3,8]{1,0:T(4,128)S(1)} %copy-done.4), custom_call_target="tpu_custom_call" | custom-call | tf_op jit(solution)/shard_map/pallas_call | solution.py:195
  24.5 0.7 %copy.9 = f32[3,16,8,128]{3,2,1,0:T(8,128)} copy(f32[3,16,8,128]{3,2,1,0:T(8,128)S(1)} %get-tuple-element.4) | data formatting | bytes 393216
  25.1 0.7 %copy.10 = f32[3,16,8,128]{3,2,1,0:T(8,128)} copy(f32[3,16,8,128]{3,2,1,0:T(8,128)S(1)} %get-tuple-element.5) | data formatting | bytes 393216
Async XLA Ops:
  0.6 0.9 %copy-start = (f32[3,16,8,128]{3,2,1,0:T(8,128)S(1)}, f32[3,16,8,128]{3,2,1,0:T(8,128)}, u32[]{:S(2)}) copy-start(f32[3,16,8,128]{3,2,1,0:T(8,128)} %pre_ref.1) | copy-start | bytes 589828
  1.6 0.9 %copy-start.1 = (f32[3,16,8,128]{3,2,1,0:T(8,128)S(1)}, f32[3,16,8,128]{3,2,1,0:T(8,128)}, u32[]{:S(2)}) copy-start(f32[3,16,8,128]{3,2,1,0:T(8,128)} %face_ref.1) | copy-start | bytes 589828
  2.5 0.8 %copy-start.2 = (s32[16,8,128]{2,1,0:T(8,128)S(1)}, s32[16,8,128]{2,1,0:T(8,128)}, u32[]{:S(2)}) copy-start(s32[16,8,128]{2,1,0:T(8,128)} %solid_ref.1) | copy-start | bytes 196612
  3.3 0.7 %copy-start.3 = (f32[3,8]{1,0:T(4,128)S(1)}, f32[3,8]{1,0:T(4,128)}, u32[]{:S(2)}) copy-start(f32[3,8]{1,0:T(4,128)} %prof_ref.1) | copy-start | bytes 292
  4.0 0.7 %copy-start.4 = (f32[3,8]{1,0:T(4,128)S(1)}, f32[3,8]{1,0:T(4,128)}, u32[]{:S(2)}) copy-start(f32[3,8]{1,0:T(4,128)} %spread_ref.1) | copy-start | bytes 292

commit v2 on v1

v2 whole, which is shorter than its diff:
```python
import functools

import jax
import jax.numpy as jnp
from jax import lax
from jax.experimental import pallas as pl
from jax.experimental.pallas import tpu as pltpu
from jax.sharding import PartitionSpec as P

STEPS = 3
UNROLL = 16
REMOTE = True

time_step = 0.3
viscosity = 0.04
smag_coef = 0.03
spread_eps = 1e-05


def stencil(u, len_dn, len_up, hgt_dn, hgt_up, wid_dn, wid_up):
    dn, up = (len_dn, hgt_dn, wid_dn), (len_up, hgt_up, wid_up)
    diff = [[up[d][c] - dn[d][c] for d in range(3)] for c in range(3)]
    diag = diff[0][0] * diff[0][0] + diff[1][1] * diff[1][1] + diff[2][2] * diff[2][2]
    s01 = diff[0][1] + diff[1][0]
    s02 = diff[0][2] + diff[2][0]
    s12 = diff[1][2] + diff[2][1]
    total = 2.0 * diag + s01 * s01 + s02 * s02 + s12 * s12
    nu = time_step * viscosity + (0.5 * time_step * smag_coef) * jnp.sqrt(total)
    half = [(0.5 * time_step) * u[d] for d in range(3)]
    out = []
    for c in range(3):
        lap = (up[0][c] + dn[0][c]) + (up[1][c] + dn[1][c]) + (up[2][c] + dn[2][c]) - 6.0 * u[c]
        adv = half[0] * diff[c][0] + half[1] * diff[c][1] + half[2] * diff[c][2]
        out.append(u[c] + nu * lap - adv)
    return out


def kernel(counts, pre_hbm, face_hbm, solid_hbm, prof_hbm, spread_hbm, pre_out, face_out,
           state, solid_ref, prof_ref, spread_ref, hsend, hrecv, wsend, wrecv, load_sem, send_sem, recv_sem):
    n_len, n_hgt, n_wid = counts
    planes, rows, cols = solid_ref.shape
    me_len, me_hgt, me_wid = lax.axis_index("len"), lax.axis_index("hgt"), lax.axis_index("wid")
    next_len = lax.rem(me_len + 1, n_len)
    prev_len = lax.rem(me_len + n_len - 1, n_len)

    partners = (
        ("len", next_len, None),
        ("len", prev_len, None),
        ("hgt", me_hgt + 1, me_hgt < n_hgt - 1),
        ("hgt", me_hgt - 1, me_hgt > 0),
        ("wid", me_wid + 1, me_wid < n_wid - 1),
        ("wid", me_wid - 1, me_wid > 0),
    )
    arrives = (None, None, me_hgt > 0, me_hgt < n_hgt - 1, me_wid > 0, me_wid < n_wid - 1)

    def guarded(cond, fn):
        if cond is None:
            fn()
        else:
            pl.when(cond)(fn)

    if REMOTE:
        barrier = pltpu.get_barrier_semaphore()
        for axis, target, cond in partners:
            guarded(cond, lambda axis=axis, target=target: pl.semaphore_signal(
                barrier, inc=1, device_id={axis: target}, device_id_type=pl.DeviceIdType.MESH))

    loads = [
        pltpu.make_async_copy(src, dst, load_sem.at[k])
        for k, (src, dst) in enumerate((
            (pre_hbm, state.at[0, 0, :, 1:planes + 1]),
            (face_hbm, state.at[0, 1, :, 1:planes + 1]),
            (prof_hbm, prof_ref),
            (spread_hbm, spread_ref),
            (solid_hbm, solid_ref),
        ))
    ]
    for copy in loads:
        copy.start()

    sub = lax.broadcasted_iota(jnp.int32, (rows, cols), 0)
    lane = lax.broadcasted_iota(jnp.int32, (rows, cols), 1)

    zero_rows = jnp.zeros(hrecv.shape[3:], jnp.float32)
    zero_cols = jnp.zeros(wrecv.shape[2:], jnp.float32)

    def no_rows(side):
        def go():
            for s in range(STEPS):
                for z in range(2):
                    hrecv[s, z, side] = zero_rows
        return go

    def no_cols(side):
        def go():
            for s in range(STEPS):
                wrecv[s, side] = zero_cols
        return go

    pl.when(me_hgt == 0)(no_rows(0))
    pl.when(me_hgt == n_hgt - 1)(no_rows(1))
    pl.when(me_wid == 0)(no_cols(0))
    pl.when(me_wid == n_wid - 1)(no_cols(1))

    def copies(s, z):
        pairs = [
            (state.at[s, z, :, planes], state.at[s, z, :, 0]),
            (state.at[s, z, :, 1], state.at[s, z, :, planes + 1]),
            (hsend.at[s, z, 1], hrecv.at[s, z, 0]),
            (hsend.at[s, z, 0], hrecv.at[s, z, 1]),
        ]
        if z == 1:
            pairs += [(wsend.at[s], wrecv.at[s, 0]), (wsend.at[s], wrecv.at[s, 1])]
        return [
            pltpu.make_async_remote_copy(
                src_ref=src, dst_ref=dst, send_sem=send_sem.at[s, z, k], recv_sem=recv_sem.at[s, z, k],
                device_id={partners[k][0]: partners[k][1]}, device_id_type=pl.DeviceIdType.MESH)
            for k, (src, dst) in enumerate(pairs)
        ]

    def start(s, z):
        if REMOTE:
            sends = copies(s, z)
            for k in reversed(range(len(sends))):
                guarded(partners[k][2], sends[k].start)

    def wait_recv(s, z):
        if REMOTE:
            for k, copy in enumerate(copies(s, z)):
                guarded(arrives[k], copy.wait_recv)

    def pack(s, z, l, x, acc):
        for c in range(3):
            hsend[s, z, 0, c, pl.ds(l, 1), :] = x[c][0:1]
            hsend[s, z, 1, c, pl.ds(l, 1), :] = x[c][rows - 1:rows]
        if z == 0:
            return acc
        mine = (lane >> 1) == l
        return [jnp.where(mine, pltpu.roll(x[c], 2 * l + 1, 1), acc[c]) for c in range(3)]

    def empty(z):
        return [jnp.zeros((rows, cols), jnp.float32)] * 3 if z == 1 else []

    def send(s, z, acc):
        for c, x in enumerate(acc):
            wsend[s, c] = x
        start(s, z)

    for z in range(2):
        loads[z].wait()

        def first(l, acc, z=z):
            return pack(0, z, l, [state[0, z, c, l + 1] for c in range(3)], acc)

        acc = lax.fori_loop(0, planes, first, empty(z), unroll=UNROLL)
        if z == 0 and REMOTE:
            expected = sum([jnp.int32(1) if cond is None else cond.astype(jnp.int32) for _, _, cond in partners])
            pl.semaphore_wait(barrier, expected)
        send(0, z, acc)

    for copy in loads[2:]:
        copy.wait()

    pick = lax.broadcasted_iota(jnp.int32, (rows, rows), 0) == lax.broadcasted_iota(jnp.int32, (rows, rows), 1)

    def column(ref, c):
        return jnp.sum(jnp.where(pick, jnp.broadcast_to(ref[c:c + 1, :], (rows, rows)), 0.0), axis=1, keepdims=True)

    profile = [column(prof_ref, c) for c in range(3)]
    target_spread = [column(spread_ref, c) for c in range(3)]

    even = (lane & 1) == 0
    for s in range(STEPS):
        for z in range(2):
            if z == 1:
                inlet = []
                for c in range(3):
                    recycled = state[s, 0, c, 0]
                    mean = jnp.sum(recycled, axis=1, keepdims=True) * (1.0 / cols)
                    fluct = recycled - mean
                    var = jnp.sum(fluct * fluct, axis=1, keepdims=True) * (1.0 / cols)
                    inlet.append(profile[c] + target_spread[c] / jnp.sqrt(var + spread_eps) * fluct)
            wait_recv(s, z)
            ghosts = []
            if z == 1:
                for c in range(3):
                    state[s, 1, c, 0] = jnp.where(me_len == 0, inlet[c], state[s, 1, c, 0])
                    state[s, 1, c, planes + 1] = jnp.where(
                        me_len == n_len - 1, state[s, 1, c, planes], state[s, 1, c, planes + 1])
                    ghosts.append(jnp.where(
                        even, pltpu.roll(wrecv[s, 1, c], cols - 1, 1), pltpu.roll(wrecv[s, 0, c], 1, 1)))

            def plane(l, acc, s=s, z=z, ghosts=ghosts):
                u = [state[s, z, c, l + 1] for c in range(3)]
                len_dn = [state[s, z, c, l] for c in range(3)]
                len_up = [state[s, z, c, l + 2] for c in range(3)]
                hgt_dn = [jnp.where(sub == 0, hrecv[s, z, 0, c, pl.ds(l, 1), :], pltpu.roll(u[c], 1, 0)) for c in range(3)]
                hgt_up = [jnp.where(sub == rows - 1, hrecv[s, z, 1, c, pl.ds(l, 1), :], pltpu.roll(u[c], rows - 1, 0)) for c in range(3)]
                edge = [pltpu.roll(ghosts[c], cols - (2 * l + 1), 1) if z == 1 else 0.0 for c in range(3)]
                wid_dn = [jnp.where(lane == 0, edge[c], pltpu.roll(u[c], 1, 1)) for c in range(3)]
                wid_up = [jnp.where(lane == cols - 1, edge[c], pltpu.roll(u[c], cols - 1, 1)) for c in range(3)]
                x = stencil(u, len_dn, len_up, hgt_dn, hgt_up, wid_dn, wid_up)
                if z == 1:
                    share = (1 - solid_ref[l]).astype(jnp.float32)
                    x = [v * share for v in x]
                for c in range(3):
                    if s == STEPS - 1:
                        (pre_out, face_out)[z][c, l] = x[c]
                    else:
                        state[s + 1, z, c, l + 1] = x[c]
                return acc if s == STEPS - 1 else pack(s + 1, z, l, x, acc)

            acc = lax.fori_loop(0, planes, plane, empty(z), unroll=UNROLL)
            if s < STEPS - 1:
                send(s + 1, z, acc)

    if REMOTE:
        for s in range(STEPS):
            for z in range(2):
                for k, copy in enumerate(copies(s, z)):
                    guarded(partners[k][2], copy.wait_send)


def on_device(counts, precursor, face, solid, inlet_profile, target_spread):
    planes, rows, cols = solid.shape
    vmem = pl.BlockSpec(memory_space=pltpu.VMEM)
    hbm = pl.BlockSpec(memory_space=pltpu.HBM)
    f32 = jnp.float32
    return pl.pallas_call(
        functools.partial(kernel, counts),
        out_shape=(jax.ShapeDtypeStruct(precursor.shape, f32), jax.ShapeDtypeStruct(face.shape, f32)),
        in_specs=[hbm] * 5,
        out_specs=(vmem, vmem),
        scratch_shapes=[
            pltpu.VMEM((STEPS, 2, 3, planes + 2, rows, cols), f32),
            pltpu.VMEM(solid.shape, solid.dtype),
            pltpu.VMEM(inlet_profile.shape, f32),
            pltpu.VMEM(target_spread.shape, f32),
            pltpu.VMEM((STEPS, 2, 2, 3, planes, cols), f32),
            pltpu.VMEM((STEPS, 2, 2, 3, planes, cols), f32),
            pltpu.VMEM((STEPS, 3, rows, cols), f32),
            pltpu.VMEM((STEPS, 2, 3, rows, cols), f32),
            pltpu.SemaphoreType.DMA((5,)),
            pltpu.SemaphoreType.DMA((STEPS, 2, 6)),
            pltpu.SemaphoreType.DMA((STEPS, 2, 6)),
        ],
        compiler_params=pltpu.CompilerParams(
            collective_id=0 if REMOTE else None, has_side_effects=True, vmem_limit_bytes=56 * 1024 * 1024),
    )(precursor, face, solid, inlet_profile, target_spread)


def solution(mesh):
    counts = (mesh.shape["len"], mesh.shape["hgt"], mesh.shape["wid"])
    return jax.shard_map(
        functools.partial(on_device, counts),
        mesh=mesh,
        in_specs=(
            P(None, "len", "hgt", None),
            P(None, "len", "hgt", "wid"),
            P("len", "hgt", "wid"),
            P(None, "hgt"),
            P(None, "hgt"),
        ),
        out_specs=(P(None, "len", "hgt", None), P(None, "len", "hgt", "wid")),
        check_vma=False,
    )
```

time: 26.1 us -> 20.4 us (0.78)
  local copies, waits for them, and re-layouts: 5.4 us -> 2.34 us
  Pallas kernels: 19.8 us -> 17.3 us
    unnamed x12 -> x4, local copies, waits for them, and re-layouts: 5.4 us -> 2.34 us
    pallas_call x1, Pallas kernels: 19.8 us -> 17.3 us  [on_device(): pl.pallas_call(functools.partial(kernel, counts), out_shape=(jax.ShapeDty...]
where the time goes in v2:
time: 20.4 us; the launch traced here: 20.3 us
  Pallas kernels  17.3 us (85%)
  local copies, waits for them, and re-layouts  2.34 us (11%)
  between operations  0.65 us (3%)
    pallas_call x1, Pallas kernels, on_device(): pl.pallas_call(functools.partial(kernel, counts), out_shape=(jax.ShapeDty...  17.3 us
    unnamed x4, local copies, waits for them, and re-layouts  2.34 us

profile of v2, /device:TPU:0, one launch (start us, length us, event | category | flops | bytes accessed | tf_op | source)
XLA Modules:
  0.0 20.3 jit_solution(13789715583476195020)
XLA Ops:
  0.6 17.3 %shard_map.68 = (f32[3,16,8,128]{3,2,1,0:T(8,128)}, f32[3,16,8,128]{3,2,1,0:T(8,128)}) custom-call(f32[3,16,8,128]{3,2,1,0:T(8,128)} %pre_hbm.1, f32[3,16,8,128]{3,2,1,0:T(8,128)} %face_hbm.1, s32[16,8,128]{2,1,0:T(8,128)} %solid_hbm.1, f32[3,8]{1,0:T(4,128)} %prof_hbm.1, f32[3,8]{1,0:T(4,128)} %spread_hbm.1), custom_call_target="tpu_custom_call" | custom-call | tf_op jit(solution)/shard_map/pallas_call | solution.py:229
  17.9 0.0 copy-start
  18.0 1.7 %copy.9 = f32[3,16,8,128]{3,2,1,0:T(8,128)} copy(f32[3,16,8,128]{3,2,1,0:T(8,128)} %get-tuple-element.4) | data formatting | bytes 393216
  19.6 0.0 copy-done
  19.6 0.7 %copy.10 = f32[3,16,8,128]{3,2,1,0:T(8,128)} copy(f32[3,16,8,128]{3,2,1,0:T(8,128)S(1)} %copy-done) | data formatting | bytes 393216
Async XLA Ops:
  17.9 1.7 %copy-start = (f32[3,16,8,128]{3,2,1,0:T(8,128)S(1)}, f32[3,16,8,128]{3,2,1,0:T(8,128)}, u32[]{:S(2)}) copy-start(f32[3,16,8,128]{3,2,1,0:T(8,128)} %get-tuple-element.5) | copy-start | bytes 589828

commit v3 on v2

--- a/solution.py
+++ b/solution.py
@@ -8,7 +8,7 @@
 from jax.sharding import PartitionSpec as P
 
 STEPS = 3
-UNROLL = 16
+PARTS = (1, 2)
 REMOTE = True
 
 time_step = 0.3
@@ -36,7 +36,7 @@
 
 
 def kernel(counts, pre_hbm, face_hbm, solid_hbm, prof_hbm, spread_hbm, pre_out, face_out,
-           state, solid_ref, prof_ref, spread_ref, hsend, hrecv, wsend, wrecv, load_sem, send_sem, recv_sem):
+           state, solid_ref, prof_ref, spread_ref, hsend, hrecv, wsend, wrecv, load_sem, out_sem, send_sem, recv_sem):
     n_len, n_hgt, n_wid = counts
     planes, rows, cols = solid_ref.shape
     me_len, me_hgt, me_wid = lax.axis_index("len"), lax.axis_index("hgt"), lax.axis_index("wid")
@@ -118,11 +118,11 @@
             for k, (src, dst) in enumerate(pairs)
         ]
 
-    def start(s, z):
+    def start(s, z, first, last):
         if REMOTE:
-            sends = copies(s, z)
-            for k in reversed(range(len(sends))):
-                guarded(partners[k][2], sends[k].start)
+            for k, copy in enumerate(copies(s, z)):
+                if first <= k < last:
+                    guarded(partners[k][2], copy.start)
 
     def wait_recv(s, z):
         if REMOTE:
@@ -144,7 +144,7 @@
     def send(s, z, acc):
         for c, x in enumerate(acc):
             wsend[s, c] = x
-        start(s, z)
+        start(s, z, 2, 6)
 
     for z in range(2):
         loads[z].wait()
@@ -152,11 +152,15 @@
         def first(l, acc, z=z):
             return pack(0, z, l, [state[0, z, c, l + 1] for c in range(3)], acc)
 
-        acc = lax.fori_loop(0, planes, first, empty(z), unroll=UNROLL)
-        if z == 0 and REMOTE:
-            expected = sum([jnp.int32(1) if cond is None else cond.astype(jnp.int32) for _, _, cond in partners])
-            pl.semaphore_wait(barrier, expected)
-        send(0, z, acc)
+        acc = lax.fori_loop(0, planes, first, empty(z), unroll=True)
+        for c, x in enumerate(acc):
+            wsend[0, c] = x
+
+    if REMOTE:
+        expected = sum([jnp.int32(1) if cond is None else cond.astype(jnp.int32) for _, _, cond in partners])
+        pl.semaphore_wait(barrier, expected)
+    for z in range(2):
+        start(0, z, 0, 6)
 
     for copy in loads[2:]:
         copy.wait()
@@ -168,6 +172,12 @@
 
     profile = [column(prof_ref, c) for c in range(3)]
     target_spread = [column(spread_ref, c) for c in range(3)]
+
+    def result(z, p):
+        part = planes // PARTS[z]
+        return pltpu.make_async_copy(
+            state.at[STEPS, z, :, p * part + 1:(p + 1) * part + 1],
+            (pre_out, face_out)[z].at[:, p * part:(p + 1) * part], out_sem.at[z, p])
 
     even = (lane & 1) == 0
     for s in range(STEPS):
@@ -204,16 +214,23 @@
                     share = (1 - solid_ref[l]).astype(jnp.float32)
                     x = [v * share for v in x]
                 for c in range(3):
-                    if s == STEPS - 1:
-                        (pre_out, face_out)[z][c, l] = x[c]
-                    else:
-                        state[s + 1, z, c, l + 1] = x[c]
+                    state[s + 1, z, c, l + 1] = x[c]
                 return acc if s == STEPS - 1 else pack(s + 1, z, l, x, acc)
 
-            acc = lax.fori_loop(0, planes, plane, empty(z), unroll=UNROLL)
             if s < STEPS - 1:
+                acc = plane(planes - 1, plane(0, empty(z)))
+                start(s + 1, z, 0, 2)
+                acc = lax.fori_loop(1, planes - 1, plane, acc, unroll=True)
                 send(s + 1, z, acc)
-
+            else:
+                part = planes // PARTS[z]
+                for p in range(PARTS[z]):
+                    lax.fori_loop(p * part, (p + 1) * part, plane, empty(z), unroll=True)
+                    result(z, p).start()
+
+    for z in range(2):
+        for p in range(PARTS[z]):
+            result(z, p).wait()
     if REMOTE:
         for s in range(STEPS):
             for z in range(2):
@@ -221,18 +238,32 @@
                     guarded(partners[k][2], copy.wait_send)
 
 
+def copy_kernel(pre_in, face_in, pre_out, face_out, held, in_sem, out_sem):
+    pairs = ((pre_in, pre_out), (face_in, face_out))
+    loads = [pltpu.make_async_copy(src.at[c], held.at[z, c], in_sem.at[z, c])
+             for z, (src, _) in enumerate(pairs) for c in range(3)]
+    stores = [pltpu.make_async_copy(held.at[z, c], dst.at[c], out_sem.at[z, c])
+              for z, (_, dst) in enumerate(pairs) for c in range(3)]
+    for load in loads:
+        load.start()
+    for load, store in zip(loads, stores):
+        load.wait()
+        store.start()
+    for store in stores:
+        store.wait()
+
+
 def on_device(counts, precursor, face, solid, inlet_profile, target_spread):
     planes, rows, cols = solid.shape
-    vmem = pl.BlockSpec(memory_space=pltpu.VMEM)
     hbm = pl.BlockSpec(memory_space=pltpu.HBM)
     f32 = jnp.float32
-    return pl.pallas_call(
+    results = pl.pallas_call(
         functools.partial(kernel, counts),
         out_shape=(jax.ShapeDtypeStruct(precursor.shape, f32), jax.ShapeDtypeStruct(face.shape, f32)),
         in_specs=[hbm] * 5,
-        out_specs=(vmem, vmem),
+        out_specs=(hbm, hbm),
         scratch_shapes=[
-            pltpu.VMEM((STEPS, 2, 3, planes + 2, rows, cols), f32),
+            pltpu.VMEM((STEPS + 1, 2, 3, planes + 2, rows, cols), f32),
             pltpu.VMEM(solid.shape, solid.dtype),
             pltpu.VMEM(inlet_profile.shape, f32),
             pltpu.VMEM(target_spread.shape, f32),
@@ -241,12 +272,21 @@
             pltpu.VMEM((STEPS, 3, rows, cols), f32),
             pltpu.VMEM((STEPS, 2, 3, rows, cols), f32),
             pltpu.SemaphoreType.DMA((5,)),
+            pltpu.SemaphoreType.DMA((2, 4)),
             pltpu.SemaphoreType.DMA((STEPS, 2, 6)),
             pltpu.SemaphoreType.DMA((STEPS, 2, 6)),
         ],
         compiler_params=pltpu.CompilerParams(
             collective_id=0 if REMOTE else None, has_side_effects=True, vmem_limit_bytes=56 * 1024 * 1024),
     )(precursor, face, solid, inlet_profile, target_spread)
+    return pl.pallas_call(
+        copy_kernel,
+        out_shape=(jax.ShapeDtypeStruct(precursor.shape, f32), jax.ShapeDtypeStruct(face.shape, f32)),
+        in_specs=[hbm] * 2,
+        out_specs=(hbm, hbm),
+        scratch_shapes=[pltpu.VMEM((2,) + precursor.shape, f32), pltpu.SemaphoreType.DMA((2, 3)), pltpu.SemaphoreType.DMA((2, 3))],
+        compiler_params=pltpu.CompilerParams(vmem_limit_bytes=56 * 1024 * 1024),
+    )(*results)
 
 
 def solution(mesh):

time: 20.4 us -> 20 us (0.980)
  local copies, waits for them, and re-layouts: 2.34 us -> 0 us
  Pallas kernels: 17.3 us -> 19.2 us
    unnamed x4 -> x0, local copies, waits for them, and re-layouts: 2.34 us -> none
    pallas_call x0 -> x1, Pallas kernels: none -> 1.73 us  [on_device(): pl.pallas_call(copy_kernel, out_shape=(jax.ShapeDtypeStruct(precursor.sha...]
where the time goes in v3:
time: 20 us; the launch traced here: 19.9 us
  Pallas kernels  19.2 us (96%)
  between operations  0.64 us (3%)
    pallas_call x1, Pallas kernels, on_device(): pl.pallas_call(functools.partial(kernel, counts), out_shape=(jax.ShapeDty...  17.5 us
    pallas_call x1, Pallas kernels, on_device(): pl.pallas_call(copy_kernel, out_shape=(jax.ShapeDtypeStruct(precursor.sha...  1.73 us

profile of v3, /device:TPU:0, one launch (start us, length us, event | category | flops | bytes accessed | tf_op | source)
XLA Modules:
  0.0 19.9 jit_solution(6784697411950967908)
XLA Ops:
  0.6 17.5 %shard_map.68 = (f32[3,16,8,128]{3,2,1,0:T(8,128)}, f32[3,16,8,128]{3,2,1,0:T(8,128)}) custom-call(f32[3,16,8,128]{3,2,1,0:T(8,128)} %pre_hbm.1, f32[3,16,8,128]{3,2,1,0:T(8,128)} %face_hbm.1, s32[16,8,128]{2,1,0:T(8,128)} %solid_hbm.1, f32[3,8]{1,0:T(4,128)} %prof_hbm.1, f32[3,8]{1,0:T(4,128)} %spread_hbm.1), custom_call_target="tpu_custom_call" | custom-call | tf_op jit(solution)/shard_map/pallas_call | solution.py:260
  18.1 1.7 %shard_map.69 = (f32[3,16,8,128]{3,2,1,0:T(8,128)}, f32[3,16,8,128]{3,2,1,0:T(8,128)}) custom-call(f32[3,16,8,128]{3,2,1,0:T(8,128)} %get-tuple-element.4.pre_in, f32[3,16,8,128]{3,2,1,0:T(8,128)} %get-tuple-element.5.face_in), custom_call_target="tpu_custom_call" | custom-call | tf_op jit(solution)/shard_map/pallas_call | solution.py:282

commit v4 on v3

--- a/solution.py
+++ b/solution.py
@@ -118,11 +118,11 @@
             for k, (src, dst) in enumerate(pairs)
         ]
 
-    def start(s, z, first, last):
+    def start(s, z):
         if REMOTE:
-            for k, copy in enumerate(copies(s, z)):
-                if first <= k < last:
-                    guarded(partners[k][2], copy.start)
+            sends = copies(s, z)
+            for k in reversed(range(len(sends))):
+                guarded(partners[k][2], sends[k].start)
 
     def wait_recv(s, z):
         if REMOTE:
@@ -144,7 +144,7 @@
     def send(s, z, acc):
         for c, x in enumerate(acc):
             wsend[s, c] = x
-        start(s, z, 2, 6)
+        start(s, z)
 
     for z in range(2):
         loads[z].wait()
@@ -160,7 +160,7 @@
         expected = sum([jnp.int32(1) if cond is None else cond.astype(jnp.int32) for _, _, cond in partners])
         pl.semaphore_wait(barrier, expected)
     for z in range(2):
-        start(0, z, 0, 6)
+        start(0, z)
 
     for copy in loads[2:]:
         copy.wait()
@@ -218,10 +218,7 @@
                 return acc if s == STEPS - 1 else pack(s + 1, z, l, x, acc)
 
             if s < STEPS - 1:
-                acc = plane(planes - 1, plane(0, empty(z)))
-                start(s + 1, z, 0, 2)
-                acc = lax.fori_loop(1, planes - 1, plane, acc, unroll=True)
-                send(s + 1, z, acc)
+                send(s + 1, z, lax.fori_loop(0, planes, plane, empty(z), unroll=True))
             else:
                 part = planes // PARTS[z]
                 for p in range(PARTS[z]):

time: 20 us -> 19.6 us (0.980)
  Pallas kernels: 19.2 us -> 18.8 us
    pallas_call x1, Pallas kernels: 17.5 us -> 17.1 us  [on_device(): pl.pallas_call(functools.partial(kernel, counts), out_shape=(jax.ShapeDty...]
where the time goes in v4:
time: 19.6 us; the launch traced here: 19.5 us
  Pallas kernels  18.8 us (96%)
  between operations  0.64 us (3%)
    pallas_call x1, Pallas kernels, on_device(): pl.pallas_call(functools.partial(kernel, counts), out_shape=(jax.ShapeDty...  17.1 us
    pallas_call x1, Pallas kernels, on_device(): pl.pallas_call(copy_kernel, out_shape=(jax.ShapeDtypeStruct(precursor.sha...  1.73 us

profile of v4, /device:TPU:0, one launch (start us, length us, event | category | flops | bytes accessed | tf_op | source)
XLA Modules:
  0.0 19.5 jit_solution(17217095843655539961)
XLA Ops:
  0.6 17.1 %shard_map.68 = (f32[3,16,8,128]{3,2,1,0:T(8,128)}, f32[3,16,8,128]{3,2,1,0:T(8,128)}) custom-call(f32[3,16,8,128]{3,2,1,0:T(8,128)} %pre_hbm.1, f32[3,16,8,128]{3,2,1,0:T(8,128)} %face_hbm.1, s32[16,8,128]{2,1,0:T(8,128)} %solid_hbm.1, f32[3,8]{1,0:T(4,128)} %prof_hbm.1, f32[3,8]{1,0:T(4,128)} %spread_hbm.1), custom_call_target="tpu_custom_call" | custom-call | tf_op jit(solution)/shard_map/pallas_call | solution.py:257
  17.7 1.7 %shard_map.69 = (f32[3,16,8,128]{3,2,1,0:T(8,128)}, f32[3,16,8,128]{3,2,1,0:T(8,128)}) custom-call(f32[3,16,8,128]{3,2,1,0:T(8,128)} %get-tuple-element.4.pre_in, f32[3,16,8,128]{3,2,1,0:T(8,128)} %get-tuple-element.5.face_in), custom_call_target="tpu_custom_call" | custom-call | tf_op jit(solution)/shard_map/pallas_call | solution.py:279

commit v5 on v4

--- a/solution.py
+++ b/solution.py
@@ -237,10 +237,8 @@
 
 def copy_kernel(pre_in, face_in, pre_out, face_out, held, in_sem, out_sem):
     pairs = ((pre_in, pre_out), (face_in, face_out))
-    loads = [pltpu.make_async_copy(src.at[c], held.at[z, c], in_sem.at[z, c])
-             for z, (src, _) in enumerate(pairs) for c in range(3)]
-    stores = [pltpu.make_async_copy(held.at[z, c], dst.at[c], out_sem.at[z, c])
-              for z, (_, dst) in enumerate(pairs) for c in range(3)]
+    loads = [pltpu.make_async_copy(src, held.at[z], in_sem.at[z, 0]) for z, (src, _) in enumerate(pairs)]
+    stores = [pltpu.make_async_copy(held.at[z], dst, out_sem.at[z, 0]) for z, (_, dst) in enumerate(pairs)]
     for load in loads:
         load.start()
     for load, store in zip(loads, stores):

time: 19.6 us -> 19.7 us (level)
  no operation moved by 1% of the time
where the time goes in v5:
time: 19.7 us; the launch traced here: 19.5 us
  Pallas kernels  18.9 us (96%)
  between operations  0.64 us (3%)
    pallas_call x1, Pallas kernels, on_device(): pl.pallas_call(functools.partial(kernel, counts), out_shape=(jax.ShapeDty...  17.1 us
    pallas_call x1, Pallas kernels, on_device(): pl.pallas_call(copy_kernel, out_shape=(jax.ShapeDtypeStruct(precursor.sha...  1.8 us

profile of v5, /device:TPU:0, one launch (start us, length us, event | category | flops | bytes accessed | tf_op | source)
XLA Modules:
  0.0 19.5 jit_solution(7478336691741698795)
XLA Ops:
  0.6 17.1 %shard_map.68 = (f32[3,16,8,128]{3,2,1,0:T(8,128)}, f32[3,16,8,128]{3,2,1,0:T(8,128)}) custom-call(f32[3,16,8,128]{3,2,1,0:T(8,128)} %pre_hbm.1, f32[3,16,8,128]{3,2,1,0:T(8,128)} %face_hbm.1, s32[16,8,128]{2,1,0:T(8,128)} %solid_hbm.1, f32[3,8]{1,0:T(4,128)} %prof_hbm.1, f32[3,8]{1,0:T(4,128)} %spread_hbm.1), custom_call_target="tpu_custom_call" | custom-call | tf_op jit(solution)/shard_map/pallas_call | solution.py:255
  17.7 1.8 %shard_map.69 = (f32[3,16,8,128]{3,2,1,0:T(8,128)}, f32[3,16,8,128]{3,2,1,0:T(8,128)}) custom-call(f32[3,16,8,128]{3,2,1,0:T(8,128)} %get-tuple-element.4.pre_in, f32[3,16,8,128]{3,2,1,0:T(8,128)} %get-tuple-element.5.face_in), custom_call_target="tpu_custom_call" | custom-call | tf_op jit(solution)/shard_map/pallas_call | solution.py:277
